TPU v7x, 32 devices: a whole 2x2x4 slice. The times are simulated.
32 devices in a mesh: dom: 2 (over core), fsdp: 16 (over z, y, x).
Axes of the slice: x: 2, y: 2, z: 4, core: 2. Of those that a mesh axis runs over, the one named last changes fastest.
Arguments:
- weights: bfloat16 [2, 16, 640, 3584], P('dom', 'fsdp'), may hold values from -6 to 6
- activations: bfloat16 [2, 2, 320, 2560], P('dom', None, 'fsdp'), may hold values from -6 to 6
- cotangents: bfloat16 [2, 2, 320, 14336], P('dom', None, 'fsdp'), may hold values from -0.3125 to 0.3125
- lengths: int32 [2, 2, 16], P('dom', None, 'fsdp'), may hold values from 1 to 20, 240 in all within a row
Outputs:
- merged: bfloat16 [16, 640, 3584], P('fsdp')
Inputs may be any that keep to these rules, and one draw needn't show every extreme that they name: In every domain and micro-batch the lengths sum to 240, and some block is full.
All inputs are finite; a program needn't handle non-finite values.
Results may differ from a plain program's by a relative error of at most 0.018.
Values may be sent and summed in bfloat16 or wider, within the bound.
A program may use at most 64 MiB of HBM per device.

v0:
```python
import jax
import jax.numpy as jnp
from jax import lax
from jax.sharding import PartitionSpec as P

damping = 0.001


def squares(pieces):
    feat_rows, cot_rows = pieces
    grad = jnp.einsum("nmsr,nmsc->mrc", feat_rows, cot_rows, preferred_element_type=jnp.float32)
    return grad * grad


def body(weights, activations, cotangents, lengths):
    devices = lax.axis_size("fsdp")
    rows = weights.shape[2]
    cols = weights.shape[3]
    batches = activations.shape[1]
    slots = activations.shape[2]
    row_blocks = activations.shape[3] // rows
    col_blocks = devices // row_blocks
    mask = (jnp.arange(slots)[None, :] < lengths[0, :, 0:1]).astype(jnp.bfloat16)
    feats = activations[0] * mask[:, :, None]
    feat_blocks = feats.reshape(batches, slots, row_blocks, rows).transpose(2, 0, 1, 3)
    feat_send = jnp.broadcast_to(
        feat_blocks[:, None], (row_blocks, col_blocks, batches, slots, rows)
    ).reshape(devices, batches, slots, rows)
    cot_blocks = cotangents[0].reshape(batches, slots, col_blocks, cols).transpose(2, 0, 1, 3)
    cot_send = jnp.broadcast_to(
        cot_blocks[None], (row_blocks, col_blocks, batches, slots, cols)
    ).reshape(devices, batches, slots, cols)
    squared = squares(
        (
            lax.all_to_all(feat_send, "fsdp", split_axis=0, concat_axis=0, tiled=True),
            lax.all_to_all(cot_send, "fsdp", split_axis=0, concat_axis=0, tiled=True),
        )
    )
    fisher = jnp.sum(squared, axis=0) / batches
    term = fisher + damping
    numer_term = term * weights[0, 0].astype(jnp.float32)
    numer, denom = (
        lax.psum(numer_term.astype(jnp.bfloat16), "dom").astype(jnp.float32),
        lax.psum(term.astype(jnp.bfloat16), "dom").astype(jnp.float32),
    )
    merged = (numer / denom).astype(jnp.bfloat16)
    return merged[None]


def solution(mesh):
    return jax.shard_map(
        body,
        mesh=mesh,
        in_specs=(
            P("dom", "fsdp", None, None),
            P("dom", None, "fsdp", None),
            P("dom", None, "fsdp", None),
            P("dom", None, "fsdp"),
        ),
        out_specs=P("fsdp", None, None),
        check_vma=False,
    )
```

profile of v0, /device:TPU:0, one launch (start us, length us, event | category | flops | bytes accessed | tf_op | source)
XLA Modules:
  0.0 222.9 jit_solution(1242726065590113371)
XLA Ops:
  6.5 0.0 copy-start
  6.5 0.8 fusion.6
  7.3 1.1 squeeze.2
  8.4 0.2 multiply_bitcast_fusion
  8.5 0.2 copy.7
  8.7 1.3 broadcast_in_dim.6
  10.0 8.3 %all-to-all-start = ((bf16[16,2,20,640]{3,1,2,0:T(2,128)(2,1)}), bf16[16,2,20,640]{3,1,2,0:T(2,128)(2,1)S(1)}, u32[]{:S(2)}, u32[]{:S(2)}) async-start(bf16[16,2,20,640]{3,1,2,0:T(2,128)(2,1)} %bitcast.2), calls=%async_computation | async-start | bytes 1638400 | tf_op jit(solution)/shard_map/all_to_all | solution.py:35
  18.3 0.0 all-reduce.3.cloned.1.call-start
  18.4 0.0 copy-done
  18.4 0.8 reshape_squeeze.3
  19.2 0.9 copy.8
  20.1 18.6 %all-to-all-done = bf16[16,2,20,640]{3,1,2,0:T(2,128)(2,1)S(1)} async-done(((bf16[16,2,20,640]{3,1,2,0:T(2,128)(2,1)}), bf16[16,2,20,640]{3,1,2,0:T(2,128)(2,1)S(1)}, u32[]{:S(2)}, u32[]{:S(2)}) %all-to-all-start) | async-done | bytes 819232 | tf_op jit(solution)/shard_map/all_to_all | solution.py:35
  38.7 4.5 %broadcast_in_dim.7 = bf16[4,4,2,20,3584]{4,2,3,1,0:T(2,128)(2,1)} broadcast(bf16[4,2,20,3584]{3,1,2,0:T(2,128)(2,1)S(1)} %copy.8), dimensions={1,2,3,4} | broadcast | bytes 5734400 | tf_op jit(solution)/shard_map/broadcast_in_dim | solution.py:30
  43.2 106.4 %all_to_all.10 = bf16[16,2,20,3584]{3,1,2,0:T(2,128)(2,1)S(1)} all-to-all(bf16[16,2,20,3584]{3,1,2,0:T(2,128)(2,1)} %bitcast.20), channel_id=1, replica_groups=mesh['dom'=2,'fsdp'=16] {'fsdp'}, dimensions={0} | all-to-all | bytes 9175040 | tf_op jit(solution)/shard_map/all_to_all | solution.py:36
  149.5 10.2 %fusion = f32[640,3584]{1,0:T(8,128)} fusion(bf16[16,2,20,3584]{3,1,2,0:T(2,128)(2,1)S(1)} %all_to_all.10, bf16[16,2,20,640]{3,1,2,0:T(2,128)(2,1)S(1)} %all-to-all-done), kind=kOutput, calls=%fused_computation.1 | convolution fusion | flops 2942894080 | bytes 14581760 | tf_op jit(solution)/shard_map/nmsr,nmsc->mrc/dot_general | solution.py:11
  159.8 10.3 %fusion.1 = (bf16[640,3584]{1,0:T(8,128)(2,1)}, bf16[640,3584]{1,0:T(8,128)(2,1)}) fusion(f32[640,3584]{1,0:T(8,128)} %fusion, bf16[1,1,640,3584]{3,2,1,0:T(8,128)(2,1)} %param.4), kind=kLoop, calls=%fused_computation.3 | loop fusion | flops 13762560 | bytes 22937600 | tf_op jit(solution)/shard_map/convert_element_type | solution.py:43
  170.1 0.0 all-reduce.3.cloned.1.call-update
  170.1 38.6 %all-reduce.3.cloned.1.call-done = (bf16[640,3584]{1,0:T(8,128)(2,1)}, bf16[640,3584]{1,0:T(8,128)(2,1)}) async-done(((bf16[640,3584]{1,0:T(8,128)(2,1)}, bf16[640,3584]{1,0:T(8,128)(2,1)}), (bf16[640,3584]{1,0:T(8,128)(2,1)}, bf16[640,3584]{1,0:T(8,128)(2,1)})) %all-reduce.3.cloned.1.call-update) | async-done | bytes 9175056 | tf_op jit(solution)/shard_map/psum | solution.py:44
  208.7 7.4 %fusion.4 = bf16[1,640,3584]{2,1,0:T(8,128)(2,1)} fusion(bf16[640,3584]{1,0:T(8,128)(2,1)} %get-tuple-element.5, bf16[640,3584]{1,0:T(8,128)(2,1)} %get-tuple-element.6), kind=kLoop, calls=%fused_computation.8 | loop fusion | flops 9175040 | bytes 13762560 | tf_op jit(solution)/shard_map/broadcast_in_dim | solution.py:47
Async XLA Ops:
  6.5 11.9 %copy-start = (bf16[1,2,20,14336]{3,1,2,0:T(2,128)(2,1)S(1)}, bf16[1,2,20,14336]{3,1,2,0:T(2,128)(2,1)}, u32[]{:S(2)}) copy-start(bf16[1,2,20,14336]{3,1,2,0:T(2,128)(2,1)} %param.6) | copy-start | bytes 3440644
  10.0 28.6 %all-to-all-start = ((bf16[16,2,20,640]{3,1,2,0:T(2,128)(2,1)}), bf16[16,2,20,640]{3,1,2,0:T(2,128)(2,1)S(1)}, u32[]{:S(2)}, u32[]{:S(2)}) async-start(bf16[16,2,20,640]{3,1,2,0:T(2,128)(2,1)} %bitcast.2), calls=%async_computation | async-start | bytes 1638400 | tf_op jit(solution)/shard_map/all_to_all | solution.py:35
  18.3 190.4 %all-reduce.3.cloned.1.call-start = ((), (), s32[]{:S(2)}) async-start(), calls=%async_computation.2 | async-start | bytes 18350080 | tf_op jit(solution)/shard_map/psum | solution.py:44
Sparse Core Ops, SparseCore 0:
  170.2 38.4 all-reduce.2
where the time goes:
time: 223 us
  blocking collectives  106 us (48%)
  waiting for transfers between devices  57.2 us (26%)
  other arithmetic  18.6 us (8%)
  between operations  13.4 us (6%)
  matrix products  10.2 us (5%)
  local copies, waits for them, and re-layouts  8.7 us (4%)
  starting transfers between devices  8.35 us (4%)
    all_to_all x1, blocking collectives, body(): lax.all_to_all(cot_send, 'fsdp', split_axis=0, concat_axis=0, tiled=True)  106 us
    psum x1, waiting for transfers between devices, body(): lax.psum(term.astype(jnp.bfloat16), 'dom').astype(jnp.float32)  38.6 us
    all_to_all x1, waiting for transfers between devices, body(): lax.all_to_all(feat_send, 'fsdp', split_axis=0, concat_axis=0, tiled=True)  18.6 us
    convert_element_type x1, other arithmetic, body(): numer_term.astype(jnp.bfloat16)  10.3 us
    dot_general x1, matrix products, squares(): jnp.einsum('nmsr,nmsc->mrc', feat_rows, cot_rows, preferred_element_type=...  10.2 us
    all_to_all x1, starting transfers between devices, body(): lax.all_to_all(feat_send, 'fsdp', split_axis=0, concat_axis=0, tiled=True)  8.31 us
    broadcast_in_dim x1, other arithmetic, body(): return merged[None]  7.38 us
    broadcast_in_dim x1, local copies, waits for them, and re-layouts, body(): jnp.broadcast_to(cot_blocks[None], (row_blocks, col_blocks, batches, slot...  4.5 us
  transfers between devices with their start and end apart: 2, of which 2 were waited for; matrix products, arithmetic and copies ran while one was open for 1% of the time, Pallas kernels for 0%

commit v1 on v0

v1 whole, which is shorter than its diff:
```python
import functools

import jax
import jax.numpy as jnp
from jax import lax
from jax.experimental import pallas as pl
from jax.experimental.pallas import tpu as pltpu
from jax.sharding import PartitionSpec as P

damping = 0.001
MESH = pl.DeviceIdType.MESH


def kernel(doms, row_blocks, col_blocks, feats, cots, weights, out, held, numer, denom, numer_in, denom_in,
           up_sem, down_sem, recv_sem, term_send, term_recv, out_send, out_recv):
    dom = lax.axis_index("dom")
    me = lax.axis_index("fsdp")
    row = lax.div(me, col_blocks)
    chunks, _, tokens, width = held.shape
    batches, rows, depth = feats.shape
    share = rows // doms
    tile = 128 if rows % 128 == 0 else rows
    piece = 64 if share % 64 == 0 else share
    last = row_blocks - 1

    barrier = pltpu.get_barrier_semaphore()
    for step in range(1, row_blocks):
        other = lax.rem(me + step * col_blocks, row_blocks * col_blocks)
        pl.semaphore_signal(barrier, inc=1, device_id=(dom, other), device_id_type=MESH)
    for step in range(1, doms):
        pl.semaphore_signal(barrier, inc=1, device_id=(lax.rem(dom + step, doms), me), device_id_type=MESH)
    pl.semaphore_wait(barrier, row_blocks - 1 + doms - 1)

    def hop(chunk, source, sem, way):
        return pltpu.make_async_remote_copy(
            src_ref=held.at[chunk, source],
            dst_ref=held.at[chunk, source],
            send_sem=sem.at[chunk, source],
            recv_sem=recv_sem.at[chunk, source],
            device_id=(dom, me + way * col_blocks),
            device_id_type=MESH,
        )

    def term_copy(chunk, peer_step, which):
        src, dst = ((numer, numer_in), (denom, denom_in))[which]
        peer = lax.rem(dom + peer_step, doms)
        return pltpu.make_async_remote_copy(
            src_ref=src.at[chunk, pl.ds(pl.multiple_of(peer * share, share), share)],
            dst_ref=dst.at[chunk, doms - 1 - peer_step],
            send_sem=term_send.at[chunk, peer_step - 1, which],
            recv_sem=term_recv.at[chunk, doms - 1 - peer_step, which],
            device_id=(peer, me),
            device_id_type=MESH,
        )

    def term_arrival(chunk, slot, which):
        dst = (numer_in, denom_in)[which]
        return pltpu.make_async_copy(dst.at[chunk, slot], dst.at[chunk, slot], term_recv.at[chunk, slot, which])

    def out_copy(chunk, peer_step):
        where = out.at[
            pl.ds(pl.multiple_of(dom * share, share), share), pl.ds(pl.multiple_of(chunk * width, width), width)
        ]
        return pltpu.make_async_remote_copy(
            src_ref=where,
            dst_ref=where,
            send_sem=out_send.at[chunk, peer_step - 1],
            recv_sem=out_recv.at[chunk, doms - 1 - peer_step],
            device_id=(lax.rem(dom + peer_step, doms), me),
            device_id_type=MESH,
        )

    def out_arrival(chunk, slot):
        peer = lax.rem(dom + slot + 1, doms)
        where = out.at[
            pl.ds(pl.multiple_of(peer * share, share), share), pl.ds(pl.multiple_of(chunk * width, width), width)
        ]
        return pltpu.make_async_copy(where, where, out_recv.at[chunk, slot])

    def compute(chunk):
        columns = pl.ds(pl.multiple_of(chunk * width, width), width)

        @pl.loop(0, rows // tile)
        def _(at):
            here = pl.ds(pl.multiple_of(at * tile, tile), tile)
            right = held[chunk].reshape(depth, width)
            total = None
            for batch in range(batches):
                grad = jnp.dot(feats[batch, here], right, preferred_element_type=jnp.float32)
                total = grad * grad if total is None else total + grad * grad
            term = total / batches + damping
            denom[chunk, here] = term.astype(jnp.bfloat16)
            numer[chunk, here] = (term * weights[here, columns].astype(jnp.float32)).astype(jnp.bfloat16)

    def merge(chunk):
        columns = pl.ds(pl.multiple_of(chunk * width, width), width)

        @pl.loop(0, share // piece)
        def _(at):
            mine = pl.ds(pl.multiple_of(dom * share + at * piece, piece), piece)
            there = pl.ds(pl.multiple_of(at * piece, piece), piece)
            top = numer[chunk, mine].astype(jnp.float32)
            low = denom[chunk, mine].astype(jnp.float32)
            for slot in range(doms - 1):
                top = top + numer_in[chunk, slot, there].astype(jnp.float32)
                low = low + denom_in[chunk, slot, there].astype(jnp.float32)
            out[mine, columns] = (top / low).astype(jnp.bfloat16)

    def inside(chunk):
        return jnp.logical_and(chunk >= 0, chunk < chunks)

    @pl.loop(0, chunks + row_blocks)
    def _(step):
        @pl.when(step < chunks)
        def _():
            held[step, row] = cots[step]

            @pl.when(row < last)
            def _():
                hop(step, row, up_sem, 1).start()

            @pl.when(row > 0)
            def _():
                hop(step, row, down_sem, -1).start()

        for far in range(1, row_blocks):
            chunk = step - far

            @pl.when(jnp.logical_and(inside(chunk), row - far >= 0))
            def _():
                hop(chunk, row - far, up_sem, 1).wait_recv()

                @pl.when(row < last)
                def _():
                    hop(chunk, row - far, up_sem, 1).start()

            @pl.when(jnp.logical_and(inside(chunk), row + far <= last))
            def _():
                hop(chunk, row + far, down_sem, -1).wait_recv()

                @pl.when(row > 0)
                def _():
                    hop(chunk, row + far, down_sem, -1).start()

        ready = step - last

        @pl.when(inside(ready))
        def _():
            compute(ready)
            for peer_step in range(1, doms):
                for which in range(2):
                    term_copy(ready, peer_step, which).start()

        before = ready - 1

        @pl.when(inside(before))
        def _():
            for slot in range(doms - 1):
                for which in range(2):
                    term_arrival(before, slot, which).wait()
            merge(before)
            for peer_step in range(1, doms):
                out_copy(before, peer_step).start()

    @pl.loop(0, chunks)
    def _(chunk):
        for source in range(row_blocks):
            @pl.when(jnp.logical_and(row < last, source <= row))
            def _():
                hop(chunk, source, up_sem, 1).wait_send()

            @pl.when(jnp.logical_and(row > 0, source >= row))
            def _():
                hop(chunk, source, down_sem, -1).wait_send()

        for peer_step in range(1, doms):
            for which in range(2):
                term_copy(chunk, peer_step, which).wait_send()
            out_copy(chunk, peer_step).wait_send()
        for slot in range(doms - 1):
            out_arrival(chunk, slot).wait()


def chunk_width(cols):
    for width in (512, 384, 256, 128):
        if cols % width == 0:
            return width
    return cols


def body(weights, activations, cotangents, lengths):
    devices = lax.axis_size("fsdp")
    doms = lax.axis_size("dom")
    rows, cols = weights.shape[2:]
    batches, slots = activations.shape[1:3]
    row_blocks = activations.shape[3] // rows
    col_blocks = devices // row_blocks
    across = [[r * col_blocks + c for c in range(col_blocks)] for r in range(row_blocks)]
    along = [[r * col_blocks + c for r in range(row_blocks)] for c in range(col_blocks)]
    width = chunk_width(cols)
    chunks = cols // width
    tokens = col_blocks * batches * slots
    depth = row_blocks * tokens

    mask = (jnp.arange(slots)[None, :] < lengths[0, :, 0:1]).astype(jnp.bfloat16)
    feats = activations[0] * mask[:, :, None]
    feats = feats.reshape(batches * slots, row_blocks, rows).transpose(1, 0, 2)
    feats = lax.all_to_all(feats, "fsdp", 0, 0, axis_index_groups=along, tiled=True)
    feats = lax.all_gather(feats, "fsdp", axis_index_groups=across)
    feats = feats.reshape(col_blocks, row_blocks, batches, slots, rows).transpose(4, 1, 0, 2, 3)
    own = jnp.arange(batches)[:, None] == jnp.arange(batches)[None, :]
    feats = jnp.where(own[:, None, None, None, :, None], feats[None], 0).reshape(batches, rows, depth)

    cots = cotangents[0].reshape(batches * slots, col_blocks, chunks, width).transpose(1, 2, 0, 3)
    cots = lax.all_to_all(cots, "fsdp", 0, 0, axis_index_groups=across, tiled=True)
    cots = cots.transpose(1, 0, 2, 3).reshape(chunks, tokens, width)

    share = rows // doms
    vmem = pl.BlockSpec(memory_space=pltpu.VMEM)
    bf16 = jnp.bfloat16
    merged = pl.pallas_call(
        functools.partial(kernel, doms, row_blocks, col_blocks),
        out_shape=jax.ShapeDtypeStruct((rows, cols), bf16),
        in_specs=[vmem] * 3,
        out_specs=vmem,
        scratch_shapes=[
            pltpu.VMEM((chunks, row_blocks, tokens, width), bf16),
            pltpu.VMEM((chunks, rows, width), bf16),
            pltpu.VMEM((chunks, rows, width), bf16),
            pltpu.VMEM((chunks, doms - 1, share, width), bf16),
            pltpu.VMEM((chunks, doms - 1, share, width), bf16),
            pltpu.SemaphoreType.DMA((chunks, row_blocks)),
            pltpu.SemaphoreType.DMA((chunks, row_blocks)),
            pltpu.SemaphoreType.DMA((chunks, row_blocks)),
            pltpu.SemaphoreType.DMA((chunks, doms - 1, 2)),
            pltpu.SemaphoreType.DMA((chunks, doms - 1, 2)),
            pltpu.SemaphoreType.DMA((chunks, doms - 1)),
            pltpu.SemaphoreType.DMA((chunks, doms - 1)),
        ],
        compiler_params=pltpu.CompilerParams(
            collective_id=0, has_side_effects=True, vmem_limit_bytes=56 << 20
        ),
    )(feats, cots, weights[0, 0])
    return merged[None]


def solution(mesh):
    return jax.shard_map(
        body,
        mesh=mesh,
        in_specs=(
            P("dom", "fsdp", None, None),
            P("dom", None, "fsdp", None),
            P("dom", None, "fsdp", None),
            P("dom", None, "fsdp"),
        ),
        out_specs=P("fsdp", None, None),
        check_vma=False,
    )
```

time: 223 us -> 140 us (0.63)
  Pallas kernels: 0 us -> 88.3 us
  blocking collectives: 106 us -> 21.4 us
  waiting for transfers between devices: 57.2 us -> 3.72 us
  other arithmetic: 18.6 us -> 2.32 us
  between operations: 13.4 us -> 0.08 us
  matrix products: 10.2 us -> 0 us
  local copies, waits for them, and re-layouts: 8.7 us -> 13.7 us
    all_to_all x1 -> x0, blocking collectives: 106 us -> none  [body(): lax.all_to_all(cot_send, 'fsdp', split_axis=0, concat_axis=0, tiled=True)]
    pallas_call x0 -> x1, Pallas kernels: none -> 88.3 us  [body(): pl.pallas_call(functools.partial(kernel, doms, row_blocks, col_blocks), o...]
    psum x1 -> x0, waiting for transfers between devices: 38.6 us -> none  [body(): lax.psum(term.astype(jnp.bfloat16), 'dom').astype(jnp.float32)]
    all_gather x0 -> x1, blocking collectives: none -> 21.4 us  [body(): feats = lax.all_gather(feats, 'fsdp', axis_index_groups=across)]
    all_to_all x1 -> x2, waiting for transfers between devices: 18.6 us -> 3.72 us  [the longest x1 3.72 us: body(): lax.all_to_all(feats, 'fsdp', 0, 0, axis_index_groups=along, tiled=True)]
    convert_element_type x1 -> x0, other arithmetic: 10.3 us -> none  [body(): numer_term.astype(jnp.bfloat16)]
    dot_general x1 -> x0, matrix products: 10.2 us -> none  [squares(): jnp.einsum('nmsr,nmsc->mrc', feat_rows, cot_rows, preferred_element_type=...]
    broadcast_in_dim x1 -> x0, other arithmetic: 7.38 us -> none  [body(): return merged[None]]
  transfers between devices with their start and end apart: 2 -> 2, of which waited for: 2 -> 1; matrix products, arithmetic and copies ran while one was open for 1% -> 5% of each run, Pallas kernels for 0% -> 0%
where the time goes in v1:
time: 140 us
  Pallas kernels  88.3 us (63%)
  blocking collectives  21.4 us (15%)
  local copies, waits for them, and re-layouts  13.7 us (10%)
  starting transfers between devices  10 us (7%)
  waiting for transfers between devices  3.72 us (3%)
  other arithmetic  2.32 us (2%)
    pallas_call x1, Pallas kernels, body(): pl.pallas_call(functools.partial(kernel, doms, row_blocks, col_blocks), o...  88.3 us
    all_gather x1, blocking collectives, body(): feats = lax.all_gather(feats, 'fsdp', axis_index_groups=across)  21.4 us
    all_to_all x1, starting transfers between devices, body(): lax.all_to_all(feats, 'fsdp', 0, 0, axis_index_groups=along, tiled=True)  6.32 us
    unnamed x5, local copies, waits for them, and re-layouts  6.05 us
    all_to_all x1, waiting for transfers between devices, body(): lax.all_to_all(feats, 'fsdp', 0, 0, axis_index_groups=along, tiled=True)  3.72 us
    all_to_all x1, starting transfers between devices, body(): lax.all_to_all(cots, 'fsdp', 0, 0, axis_index_groups=across, tiled=True)  3.72 us
  transfers between devices with their start and end apart: 2, of which 1 were waited for; matrix products, arithmetic and copies ran while one was open for 5% of the time, Pallas kernels for 0%

profile of v1, /device:TPU:0, one launch (start us, length us, event | category | flops | bytes accessed | tf_op | source)
XLA Modules:
  0.0 139.5 jit_solution(1303319768770172463)
XLA Ops:
  0.0 0.0 copy-start
  0.0 0.8 compare_convert_fusion
  0.8 0.1 reshape.52
  0.9 1.0 copy.10
  1.9 0.1 squeeze.7
  1.9 0.2 multiply_bitcast_fusion
  2.1 0.7 copy.11
  2.8 6.3 %all-to-all-start = ((bf16[4,40,640]{2,1,0:T(8,128)(2,1)}), bf16[4,40,640]{2,1,0:T(8,128)(2,1)S(1)}, u32[]{:S(2)}, u32[]{:S(2)}) async-start(bf16[4,40,640]{2,1,0:T(8,128)(2,1)} %copy.11), calls=%async_computation | async-start | bytes 409600 | tf_op jit(solution)/shard_map/all_to_all | solution.py:208
  9.1 0.0 copy-done
  9.1 0.3 copy.15
  9.5 1.9 %reshape_squeeze.3 = bf16[40,4,7,512]{3,2,1,0:T(8,128)(2,1)S(1)} reshape(bf16[1,2,20,14336]{3,2,1,0:T(8,128)(2,1)S(1)} %copy.15) | data formatting | bytes 2293760 | tf_op jit(solution)/shard_map/reshape;squeeze | solution.py:214
  11.4 1.7 %copy.16 = bf16[4,7,40,512]{3,2,1,0:T(8,128)(2,1)} copy(bf16[4,7,40,512]{3,1,0,2:T(8,128)(2,1)S(1)} %bitcast.14) | data formatting | bytes 2293760 | tf_op jit(solution)/shard_map/transpose | solution.py:214
  13.1 3.7 %all-to-all-done = bf16[4,40,640]{2,1,0:T(8,128)(2,1)S(1)} async-done(((bf16[4,40,640]{2,1,0:T(8,128)(2,1)}), bf16[4,40,640]{2,1,0:T(8,128)(2,1)S(1)}, u32[]{:S(2)}, u32[]{:S(2)}) %all-to-all-start) | async-done | bytes 204832 | tf_op jit(solution)/shard_map/all_to_all | solution.py:208
  16.8 3.7 %all-to-all-start.1 = ((bf16[4,7,40,512]{3,2,1,0:T(8,128)(2,1)}), bf16[4,7,40,512]{3,2,1,0:T(8,128)(2,1)S(1)}, u32[]{:S(2)}, u32[]{:S(2)}) async-start(bf16[4,7,40,512]{3,2,1,0:T(8,128)(2,1)} %copy.16), calls=%async_computation.1 | async-start | bytes 2293760 | tf_op jit(solution)/shard_map/all_to_all | solution.py:215
  20.6 0.1 broadcast_in_dim.35
  20.6 0.1 broadcast_in_dim.36
  20.8 21.4 %all-gather = bf16[16,40,640]{2,1,0:T(8,128)(2,1)S(1)} all-gather(bf16[4,40,640]{2,1,0:T(8,128)(2,1)S(1)} %all-to-all-done), channel_id=2, replica_groups={{0,1,2,3},{4,5,6,7},{8,9,10,11},{12,13,14,15},{16,17,18,19},{20,21,22,2..., dimensions={0}, use_global_device_ids=true | all-gather | bytes 1024000 | tf_op jit(solution)/shard_map/all_gather | solution.py:209
  42.2 0.2 reshape.55
  42.4 0.3 copy.20
  42.7 0.2 copy.13
  42.9 0.2 broadcast_in_dim.38
  43.0 0.9 copy.14
  44.0 1.3 broadcast_select_fusion.feats
  45.3 0.0 all-to-all-done.1
  45.3 1.2 copy.17
  46.5 88.3 %shard_map.46 = bf16[640,3584]{1,0:T(8,128)(2,1)} custom-call(bf16[2,640,640]{2,1,0:T(8,128)(2,1)} %broadcast_select_fusion.feats, bf16[7,160,512]{2,1,0:T(8,128)(2,1)} %bitcast.15, bf16[640,3584]{1,0:T(8,128)(2,1)} %bitcast.17), custom_call_target="tpu_custom_call" | custom-call | tf_op jit(solution)/shard_map/pallas_call | solution.py:221
  134.8 4.7 %copy.22 = bf16[1,640,3584]{2,1,0:T(8,128)(2,1)} copy(bf16[1,640,3584]{2,1,0:T(8,128)(2,1)} %bitcast.13) | data formatting | bytes 9175040
  (1 shorter events, 0.0 us)
Async XLA Ops:
  0.0 9.1 %copy-start = (bf16[1,2,20,14336]{3,1,2,0:T(2,128)(2,1)S(1)}, bf16[1,2,20,14336]{3,1,2,0:T(2,128)(2,1)}, u32[]{:S(2)}) copy-start(bf16[1,2,20,14336]{3,1,2,0:T(2,128)(2,1)} %param.6) | copy-start | bytes 3440644
  2.8 14.0 %all-to-all-start = ((bf16[4,40,640]{2,1,0:T(8,128)(2,1)}), bf16[4,40,640]{2,1,0:T(8,128)(2,1)S(1)}, u32[]{:S(2)}, u32[]{:S(2)}) async-start(bf16[4,40,640]{2,1,0:T(8,128)(2,1)} %copy.11), calls=%async_computation | async-start | bytes 409600 | tf_op jit(solution)/shard_map/all_to_all | solution.py:208
  16.8 28.5 %all-to-all-start.1 = ((bf16[4,7,40,512]{3,2,1,0:T(8,128)(2,1)}), bf16[4,7,40,512]{3,2,1,0:T(8,128)(2,1)S(1)}, u32[]{:S(2)}, u32[]{:S(2)}) async-start(bf16[4,7,40,512]{3,2,1,0:T(8,128)(2,1)} %copy.16), calls=%async_computation.1 | async-start | bytes 2293760 | tf_op jit(solution)/shard_map/all_to_all | solution.py:215

commit v2 on v1

--- a/solution.py
+++ b/solution.py
@@ -11,25 +11,97 @@
 MESH = pl.DeviceIdType.MESH
 
 
-def kernel(doms, row_blocks, col_blocks, feats, cots, weights, out, held, numer, denom, numer_in, denom_in,
-           up_sem, down_sem, recv_sem, term_send, term_recv, out_send, out_recv):
+def kernel(doms, row_blocks, col_blocks, live, feats, cots, weights, out, feat_box, feat_all, feat_rows, feat_cols,
+           inbox, held, numer, denom, numer_in, denom_in, along_send, along_recv, across_send, across_recv,
+           piece_send, piece_recv, up_sem, down_sem, recv_sem, term_send, term_recv, out_send, out_recv):
     dom = lax.axis_index("dom")
     me = lax.axis_index("fsdp")
     row = lax.div(me, col_blocks)
+    col = lax.rem(me, col_blocks)
     chunks, _, tokens, width = held.shape
-    batches, rows, depth = feats.shape
+    batches, rows, depth = feat_cols.shape
     share = rows // doms
     tile = 128 if rows % 128 == 0 else rows
     piece = 64 if share % 64 == 0 else share
+    strip = 128 if depth % 128 == 0 else depth
     last = row_blocks - 1
 
     barrier = pltpu.get_barrier_semaphore()
     for step in range(1, row_blocks):
         other = lax.rem(me + step * col_blocks, row_blocks * col_blocks)
         pl.semaphore_signal(barrier, inc=1, device_id=(dom, other), device_id_type=MESH)
+    for step in range(1, col_blocks):
+        other = row * col_blocks + lax.rem(col + step, col_blocks)
+        pl.semaphore_signal(barrier, inc=1, device_id=(dom, other), device_id_type=MESH)
     for step in range(1, doms):
         pl.semaphore_signal(barrier, inc=1, device_id=(lax.rem(dom + step, doms), me), device_id_type=MESH)
-    pl.semaphore_wait(barrier, row_blocks - 1 + doms - 1)
+    pl.semaphore_wait(barrier, row_blocks - 1 + col_blocks - 1 + doms - 1)
+
+    def feat_along(step):
+        peer = lax.rem(row + step, row_blocks)
+        return pltpu.make_async_remote_copy(
+            src_ref=feats.at[peer],
+            dst_ref=feat_box.at[row],
+            send_sem=along_send.at[step - 1],
+            recv_sem=along_recv.at[row_blocks - 1 - step],
+            device_id=(dom, peer * col_blocks + col),
+            device_id_type=MESH,
+        )
+
+    def feat_along_arrival(slot):
+        dst = feat_box.at[lax.rem(row + slot + 1, row_blocks)]
+        return pltpu.make_async_copy(dst, dst, along_recv.at[slot])
+
+    def feat_across(step):
+        return pltpu.make_async_remote_copy(
+            src_ref=feat_box,
+            dst_ref=feat_all.at[col_blocks - 1 - step],
+            send_sem=across_send.at[step - 1],
+            recv_sem=across_recv.at[col_blocks - 1 - step],
+            device_id=(dom, row * col_blocks + lax.rem(col + step, col_blocks)),
+            device_id_type=MESH,
+        )
+
+    def feat_across_arrival(slot):
+        dst = feat_all.at[slot]
+        return pltpu.make_async_copy(dst, dst, across_recv.at[slot])
+
+    def piece_copy(chunk, step):
+        peer = lax.rem(col + step, col_blocks)
+        return pltpu.make_async_remote_copy(
+            src_ref=cots.at[peer, chunk],
+            dst_ref=inbox.at[chunk, col_blocks - 1 - step],
+            send_sem=piece_send.at[chunk, step - 1],
+            recv_sem=piece_recv.at[chunk, col_blocks - 1 - step],
+            device_id=(dom, row * col_blocks + peer),
+            device_id_type=MESH,
+        )
+
+    def piece_arrival(chunk, slot):
+        dst = inbox.at[chunk, slot]
+        return pltpu.make_async_copy(dst, dst, piece_recv.at[chunk, slot])
+
+    def join(parts):
+        return jnp.concatenate([part.astype(jnp.float32)[:live] for part in parts], axis=0)
+
+    def assemble(chunk):
+        parts = [cots[col, chunk]] + [inbox[chunk, slot] for slot in range(col_blocks - 1)]
+        held[chunk, row] = join(parts).astype(jnp.bfloat16)
+
+    def turn_feats():
+        @pl.loop(0, row_blocks)
+        def _(at):
+            parts = [feat_box[at]] + [feat_all[slot, at] for slot in range(col_blocks - 1)]
+            feat_rows[pl.ds(pl.multiple_of(at * tokens, tokens), tokens)] = join(parts)
+
+        @pl.loop(0, depth // strip)
+        def _(at):
+            here = pl.ds(pl.multiple_of(at * strip, strip), strip)
+            turned = feat_rows[here].T
+            token = lax.broadcasted_iota(jnp.int32, (rows, strip), 1) + at * strip
+            owner = lax.div(lax.rem(token, live), live // batches)
+            for batch in range(batches):
+                feat_cols[batch, :, here] = jnp.where(owner == batch, turned, 0.0).astype(jnp.bfloat16)
 
     def hop(chunk, source, sem, way):
         return pltpu.make_async_remote_copy(
@@ -86,7 +158,7 @@
             right = held[chunk].reshape(depth, width)
             total = None
             for batch in range(batches):
-                grad = jnp.dot(feats[batch, here], right, preferred_element_type=jnp.float32)
+                grad = jnp.dot(feat_cols[batch, here], right, preferred_element_type=jnp.float32)
                 total = grad * grad if total is None else total + grad * grad
             term = total / batches + damping
             denom[chunk, here] = term.astype(jnp.bfloat16)
@@ -109,11 +181,26 @@
     def inside(chunk):
         return jnp.logical_and(chunk >= 0, chunk < chunks)
 
+    ahead = min(2, chunks)
+    for step in range(1, row_blocks):
+        feat_along(step).start()
+    for chunk in range(ahead):
+        for step in range(1, col_blocks):
+            piece_copy(chunk, step).start()
+    feat_box[row] = feats[row]
+
     @pl.loop(0, chunks + row_blocks)
     def _(step):
+        @pl.when(step + ahead < chunks)
+        def _():
+            for peer_step in range(1, col_blocks):
+                piece_copy(step + ahead, peer_step).start()
+
         @pl.when(step < chunks)
         def _():
-            held[step, row] = cots[step]
+            for slot in range(col_blocks - 1):
+                piece_arrival(step, slot).wait()
+            assemble(step)
 
             @pl.when(row < last)
             def _():
@@ -122,6 +209,13 @@
             @pl.when(row > 0)
             def _():
                 hop(step, row, down_sem, -1).start()
+
+        @pl.when(step == 0)
+        def _():
+            for slot in range(row_blocks - 1):
+                feat_along_arrival(slot).wait()
+            for peer_step in range(1, col_blocks):
+                feat_across(peer_step).start()
 
         for far in range(1, row_blocks):
             chunk = step - far
@@ -143,6 +237,12 @@
                     hop(chunk, row + far, down_sem, -1).start()
 
         ready = step - last
+
+        @pl.when(ready == 0)
+        def _():
+            for slot in range(col_blocks - 1):
+                feat_across_arrival(slot).wait()
+            turn_feats()
 
         @pl.when(inside(ready))
         def _():
@@ -162,8 +262,15 @@
             for peer_step in range(1, doms):
                 out_copy(before, peer_step).start()
 
+    for step in range(1, row_blocks):
+        feat_along(step).wait_send()
+    for step in range(1, col_blocks):
+        feat_across(step).wait_send()
+
     @pl.loop(0, chunks)
     def _(chunk):
+        for step in range(1, col_blocks):
+            piece_copy(chunk, step).wait_send()
         for source in range(row_blocks):
             @pl.when(jnp.logical_and(row < last, source <= row))
             def _():
@@ -195,8 +302,6 @@
     batches, slots = activations.shape[1:3]
     row_blocks = activations.shape[3] // rows
     col_blocks = devices // row_blocks
-    across = [[r * col_blocks + c for c in range(col_blocks)] for r in range(row_blocks)]
-    along = [[r * col_blocks + c for r in range(row_blocks)] for c in range(col_blocks)]
     width = chunk_width(cols)
     chunks = cols // width
     tokens = col_blocks * batches * slots
@@ -204,31 +309,38 @@
 
     mask = (jnp.arange(slots)[None, :] < lengths[0, :, 0:1]).astype(jnp.bfloat16)
     feats = activations[0] * mask[:, :, None]
-    feats = feats.reshape(batches * slots, row_blocks, rows).transpose(1, 0, 2)
-    feats = lax.all_to_all(feats, "fsdp", 0, 0, axis_index_groups=along, tiled=True)
-    feats = lax.all_gather(feats, "fsdp", axis_index_groups=across)
-    feats = feats.reshape(col_blocks, row_blocks, batches, slots, rows).transpose(4, 1, 0, 2, 3)
-    own = jnp.arange(batches)[:, None] == jnp.arange(batches)[None, :]
-    feats = jnp.where(own[:, None, None, None, :, None], feats[None], 0).reshape(batches, rows, depth)
-
-    cots = cotangents[0].reshape(batches * slots, col_blocks, chunks, width).transpose(1, 2, 0, 3)
-    cots = lax.all_to_all(cots, "fsdp", 0, 0, axis_index_groups=across, tiled=True)
-    cots = cots.transpose(1, 0, 2, 3).reshape(chunks, tokens, width)
+    live = batches * slots
+    padded = -(-live // 16) * 16
+    feats = feats.reshape(live, row_blocks, rows)
+    feats = jnp.pad(feats, ((0, padded - live), (0, 0), (0, 0))).transpose(1, 0, 2)
+    cots = cotangents[0].reshape(live, col_blocks, chunks, width)
+    cots = jnp.pad(cots, ((0, padded - live), (0, 0), (0, 0), (0, 0))).transpose(1, 2, 0, 3)
 
     share = rows // doms
     vmem = pl.BlockSpec(memory_space=pltpu.VMEM)
     bf16 = jnp.bfloat16
     merged = pl.pallas_call(
-        functools.partial(kernel, doms, row_blocks, col_blocks),
+        functools.partial(kernel, doms, row_blocks, col_blocks, live),
         out_shape=jax.ShapeDtypeStruct((rows, cols), bf16),
         in_specs=[vmem] * 3,
         out_specs=vmem,
         scratch_shapes=[
+            pltpu.VMEM((row_blocks, padded, rows), bf16),
+            pltpu.VMEM((col_blocks - 1, row_blocks, padded, rows), bf16),
+            pltpu.VMEM((depth, rows), jnp.float32),
+            pltpu.VMEM((batches, rows, depth), bf16),
+            pltpu.VMEM((chunks, col_blocks - 1, padded, width), bf16),
             pltpu.VMEM((chunks, row_blocks, tokens, width), bf16),
             pltpu.VMEM((chunks, rows, width), bf16),
             pltpu.VMEM((chunks, rows, width), bf16),
             pltpu.VMEM((chunks, doms - 1, share, width), bf16),
             pltpu.VMEM((chunks, doms - 1, share, width), bf16),
+            pltpu.SemaphoreType.DMA((row_blocks - 1,)),
+            pltpu.SemaphoreType.DMA((row_blocks - 1,)),
+            pltpu.SemaphoreType.DMA((col_blocks - 1,)),
+            pltpu.SemaphoreType.DMA((col_blocks - 1,)),
+            pltpu.SemaphoreType.DMA((chunks, col_blocks - 1)),
+            pltpu.SemaphoreType.DMA((chunks, col_blocks - 1)),
             pltpu.SemaphoreType.DMA((chunks, row_blocks)),
             pltpu.SemaphoreType.DMA((chunks, row_blocks)),
             pltpu.SemaphoreType.DMA((chunks, row_blocks)),

time: 140 us -> 109 us (0.78)
  blocking collectives: 21.4 us -> 0 us
  starting transfers between devices: 10 us -> 0 us
  Pallas kernels: 88.3 us -> 96.9 us
  waiting for transfers between devices: 3.72 us -> 0 us
  local copies, waits for them, and re-layouts: 13.7 us -> 10.8 us
  other arithmetic: 2.32 us -> 0.91 us
    all_gather x1 -> x0, blocking collectives: 21.4 us -> none  [body(): feats = lax.all_gather(feats, 'fsdp', axis_index_groups=across)]
    all_to_all x2 -> x0, starting transfers between devices: 10 us -> none  [the longest x1 6.32 us: body(): lax.all_to_all(feats, 'fsdp', 0, 0, axis_index_groups=along, tiled=True)]
    pallas_call x1, Pallas kernels: 88.3 us -> 96.9 us  [body(): pl.pallas_call(functools.partial(kernel, doms, row_blocks, col_blocks, li...]
    all_to_all x2 -> x0, waiting for transfers between devices: 3.72 us -> none  [the longest x1 3.72 us: body(): lax.all_to_all(feats, 'fsdp', 0, 0, axis_index_groups=along, tiled=True)]
    transpose x4 -> x2, local copies, waits for them, and re-layouts: 3.79 us -> 1.96 us  [the longest x1 1.24 us: body(): jnp.pad(cots, ((0, padded - live), (0, 0), (0, 0), (0, 0)))]
  transfers between devices with their start and end apart: 2 -> 0, of which waited for: 1 -> 0; matrix products, arithmetic and copies ran while one was open for 5% -> 0% of each run, Pallas kernels for 0% -> 0%
where the time goes in v2:
time: 109 us
  Pallas kernels  96.9 us (89%)
  local copies, waits for them, and re-layouts  10.8 us (10%)
    pallas_call x1, Pallas kernels, body(): pl.pallas_call(functools.partial(kernel, doms, row_blocks, col_blocks, li...  96.9 us
    unnamed x5, local copies, waits for them, and re-layouts  6.05 us
    another operation x2, local copies, waits for them, and re-layouts, body(): cots = cotangents[0].reshape(live, col_blocks, chunks, width)  2.6 us

profile of v2, /device:TPU:0, one launch (start us, length us, event | category | flops | bytes accessed | tf_op | source)
XLA Modules:
  0.0 108.6 jit_solution(8009467356422841251)
XLA Ops:
  0.0 0.0 copy-start
  0.0 0.8 compare_convert_fusion
  0.8 0.1 reshape.27
  0.9 1.0 copy.5
  1.9 0.1 squeeze.7
  1.9 0.1 copy_multiply_fusion
  2.0 0.7 pad_bitcast_fusion.1.feats
  2.8 0.0 copy-done
  2.8 0.3 copy.7
  3.1 1.9 %reshape_squeeze.3 = bf16[40,4,7,512]{3,2,1,0:T(8,128)(2,1)S(1)} reshape(bf16[1,2,20,14336]{3,2,1,0:T(8,128)(2,1)S(1)} %copy.7) | data formatting | bytes 2293760 | tf_op jit(solution)/shard_map/reshape;squeeze | solution.py:316
  5.0 0.7 copy.8
  5.7 1.2 %pad_bitcast_fusion.cots = bf16[4,7,48,512]{3,2,1,0:T(8,128)(2,1)} fusion(bf16[40,4,7,512]{3,0,2,1:T(8,128)(2,1)S(1)} %copy.8), kind=kLoop, calls=%fused_computation | loop fusion | bytes 2523136 | tf_op jit(solution)/shard_map/transpose | solution.py:317
  7.0 96.9 %shard_map.46 = bf16[640,3584]{1,0:T(8,128)(2,1)} custom-call(bf16[4,48,640]{2,1,0:T(8,128)(2,1)} %pad_bitcast_fusion.1.feats, bf16[4,7,48,512]{3,2,1,0:T(8,128)(2,1)} %pad_bitcast_fusion.cots, bf16[640,3584]{1,0:T(8,128)(2,1)} %bitcast.8), custom_call_target="tpu_custom_call" | custom-call | tf_op jit(solution)/shard_map/pallas_call | solution.py:322
  103.9 4.7 %copy.11 = bf16[1,640,3584]{2,1,0:T(8,128)(2,1)} copy(bf16[1,640,3584]{2,1,0:T(8,128)(2,1)} %bitcast.7) | data formatting | bytes 9175040
Async XLA Ops:
  0.0 2.8 %copy-start = (bf16[1,2,20,14336]{3,1,2,0:T(2,128)(2,1)S(1)}, bf16[1,2,20,14336]{3,1,2,0:T(2,128)(2,1)}, u32[]{:S(2)}) copy-start(bf16[1,2,20,14336]{3,1,2,0:T(2,128)(2,1)} %param.6) | copy-start | bytes 3440644

commit v3 on v2

--- a/solution.py
+++ b/solution.py
@@ -11,8 +11,9 @@
 MESH = pl.DeviceIdType.MESH
 
 
-def kernel(doms, row_blocks, col_blocks, live, feats, cots, weights, out, feat_box, feat_all, feat_rows, feat_cols,
-           inbox, held, numer, denom, numer_in, denom_in, along_send, along_recv, across_send, across_recv,
+def kernel(doms, row_blocks, col_blocks, live, feats, cots, weights_hbm, out, weights, feat_out, pieces, done,
+           feat_box, feat_all, feat_rows, feat_cols, inbox, held, numer, denom, numer_in, denom_in,
+           weight_sem, done_sem, along_send, along_recv, across_send, across_recv,
            piece_send, piece_recv, up_sem, down_sem, recv_sem, term_send, term_recv, out_send, out_recv):
     dom = lax.axis_index("dom")
     me = lax.axis_index("fsdp")
@@ -25,6 +26,13 @@
     piece = 64 if share % 64 == 0 else share
     strip = 128 if depth % 128 == 0 else depth
     last = row_blocks - 1
+    cols = chunks * width
+    padded = pieces.shape[2]
+
+    def fetch():
+        return pltpu.make_async_copy(weights_hbm, weights, weight_sem)
+
+    fetch().start()
 
     barrier = pltpu.get_barrier_semaphore()
     for step in range(1, row_blocks):
@@ -40,7 +48,7 @@
     def feat_along(step):
         peer = lax.rem(row + step, row_blocks)
         return pltpu.make_async_remote_copy(
-            src_ref=feats.at[peer],
+            src_ref=feat_out.at[peer],
             dst_ref=feat_box.at[row],
             send_sem=along_send.at[step - 1],
             recv_sem=along_recv.at[row_blocks - 1 - step],
@@ -69,7 +77,7 @@
     def piece_copy(chunk, step):
         peer = lax.rem(col + step, col_blocks)
         return pltpu.make_async_remote_copy(
-            src_ref=cots.at[peer, chunk],
+            src_ref=pieces.at[chunk, step - 1],
             dst_ref=inbox.at[chunk, col_blocks - 1 - step],
             send_sem=piece_send.at[chunk, step - 1],
             recv_sem=piece_recv.at[chunk, col_blocks - 1 - step],
@@ -84,8 +92,25 @@
     def join(parts):
         return jnp.concatenate([part.astype(jnp.float32)[:live] for part in parts], axis=0)
 
+    def pad(part):
+        if padded == live:
+            return part
+        blank = jnp.zeros((padded - live, part.shape[1]), jnp.float32)
+        return jnp.concatenate([part.astype(jnp.float32), blank], axis=0).astype(jnp.bfloat16)
+
+    def cot_part(chunk, block):
+        return cots[:, pl.ds(pl.multiple_of(block * cols + chunk * width, width), width)]
+
+    def feat_part(block):
+        return pad(feats[:, pl.ds(pl.multiple_of(block * rows, rows), rows)])
+
+    def send_pieces(chunk):
+        for step in range(1, col_blocks):
+            pieces[chunk, step - 1] = pad(cot_part(chunk, lax.rem(col + step, col_blocks)))
+            piece_copy(chunk, step).start()
+
     def assemble(chunk):
-        parts = [cots[col, chunk]] + [inbox[chunk, slot] for slot in range(col_blocks - 1)]
+        parts = [cot_part(chunk, col)] + [inbox[chunk, slot] for slot in range(col_blocks - 1)]
         held[chunk, row] = join(parts).astype(jnp.bfloat16)
 
     def turn_feats():
@@ -99,7 +124,7 @@
             here = pl.ds(pl.multiple_of(at * strip, strip), strip)
             turned = feat_rows[here].T
             token = lax.broadcasted_iota(jnp.int32, (rows, strip), 1) + at * strip
-            owner = lax.div(lax.rem(token, live), live // batches)
+            owner = lax.rem(lax.rem(token, live), batches)
             for batch in range(batches):
                 feat_cols[batch, :, here] = jnp.where(owner == batch, turned, 0.0).astype(jnp.bfloat16)
 
@@ -129,13 +154,18 @@
         dst = (numer_in, denom_in)[which]
         return pltpu.make_async_copy(dst.at[chunk, slot], dst.at[chunk, slot], term_recv.at[chunk, slot, which])
 
+    def place(owner, chunk):
+        return out.at[
+            pl.ds(pl.multiple_of(owner * share, share), share), pl.ds(pl.multiple_of(chunk * width, width), width)
+        ]
+
+    def keep(chunk):
+        return pltpu.make_async_copy(done.at[chunk], place(dom, chunk), done_sem.at[chunk])
+
     def out_copy(chunk, peer_step):
-        where = out.at[
-            pl.ds(pl.multiple_of(dom * share, share), share), pl.ds(pl.multiple_of(chunk * width, width), width)
-        ]
-        return pltpu.make_async_remote_copy(
-            src_ref=where,
-            dst_ref=where,
+        return pltpu.make_async_remote_copy(
+            src_ref=done.at[chunk],
+            dst_ref=place(dom, chunk),
             send_sem=out_send.at[chunk, peer_step - 1],
             recv_sem=out_recv.at[chunk, doms - 1 - peer_step],
             device_id=(lax.rem(dom + peer_step, doms), me),
@@ -143,10 +173,7 @@
         )
 
     def out_arrival(chunk, slot):
-        peer = lax.rem(dom + slot + 1, doms)
-        where = out.at[
-            pl.ds(pl.multiple_of(peer * share, share), share), pl.ds(pl.multiple_of(chunk * width, width), width)
-        ]
+        where = place(lax.rem(dom + slot + 1, doms), chunk)
         return pltpu.make_async_copy(where, where, out_recv.at[chunk, slot])
 
     def compute(chunk):
@@ -165,8 +192,6 @@
             numer[chunk, here] = (term * weights[here, columns].astype(jnp.float32)).astype(jnp.bfloat16)
 
     def merge(chunk):
-        columns = pl.ds(pl.multiple_of(chunk * width, width), width)
-
         @pl.loop(0, share // piece)
         def _(at):
             mine = pl.ds(pl.multiple_of(dom * share + at * piece, piece), piece)
@@ -176,25 +201,25 @@
             for slot in range(doms - 1):
                 top = top + numer_in[chunk, slot, there].astype(jnp.float32)
                 low = low + denom_in[chunk, slot, there].astype(jnp.float32)
-            out[mine, columns] = (top / low).astype(jnp.bfloat16)
+            done[chunk, there] = (top / low).astype(jnp.bfloat16)
 
     def inside(chunk):
         return jnp.logical_and(chunk >= 0, chunk < chunks)
 
     ahead = min(2, chunks)
     for step in range(1, row_blocks):
+        peer = lax.rem(row + step, row_blocks)
+        feat_out[peer] = feat_part(peer)
         feat_along(step).start()
     for chunk in range(ahead):
-        for step in range(1, col_blocks):
-            piece_copy(chunk, step).start()
-    feat_box[row] = feats[row]
+        send_pieces(chunk)
+    feat_box[row] = feat_part(row)
 
     @pl.loop(0, chunks + row_blocks)
     def _(step):
         @pl.when(step + ahead < chunks)
         def _():
-            for peer_step in range(1, col_blocks):
-                piece_copy(step + ahead, peer_step).start()
+            send_pieces(step + ahead)
 
         @pl.when(step < chunks)
         def _():
@@ -243,6 +268,7 @@
             for slot in range(col_blocks - 1):
                 feat_across_arrival(slot).wait()
             turn_feats()
+            fetch().wait()
 
         @pl.when(inside(ready))
         def _():
@@ -259,6 +285,7 @@
                 for which in range(2):
                     term_arrival(before, slot, which).wait()
             merge(before)
+            keep(before).start()
             for peer_step in range(1, doms):
                 out_copy(before, peer_step).start()
 
@@ -284,12 +311,13 @@
             for which in range(2):
                 term_copy(chunk, peer_step, which).wait_send()
             out_copy(chunk, peer_step).wait_send()
+        keep(chunk).wait()
         for slot in range(doms - 1):
             out_arrival(chunk, slot).wait()
 
 
 def chunk_width(cols):
-    for width in (512, 384, 256, 128):
+    for width in (256, 128):
         if cols % width == 0:
             return width
     return cols
@@ -307,14 +335,11 @@
     tokens = col_blocks * batches * slots
     depth = row_blocks * tokens
 
-    mask = (jnp.arange(slots)[None, :] < lengths[0, :, 0:1]).astype(jnp.bfloat16)
-    feats = activations[0] * mask[:, :, None]
+    mask = (jnp.arange(slots)[:, None] < lengths[0, :, 0][None, :]).astype(jnp.bfloat16)
     live = batches * slots
     padded = -(-live // 16) * 16
-    feats = feats.reshape(live, row_blocks, rows)
-    feats = jnp.pad(feats, ((0, padded - live), (0, 0), (0, 0))).transpose(1, 0, 2)
-    cots = cotangents[0].reshape(live, col_blocks, chunks, width)
-    cots = jnp.pad(cots, ((0, padded - live), (0, 0), (0, 0), (0, 0))).transpose(1, 2, 0, 3)
+    feats = (activations[0].transpose(1, 0, 2) * mask[:, :, None]).reshape(live, row_blocks * rows)
+    cots = cotangents[0].transpose(1, 0, 2).reshape(live, col_blocks * cols)
 
     share = rows // doms
     vmem = pl.BlockSpec(memory_space=pltpu.VMEM)
@@ -322,9 +347,13 @@
     merged = pl.pallas_call(
         functools.partial(kernel, doms, row_blocks, col_blocks, live),
         out_shape=jax.ShapeDtypeStruct((rows, cols), bf16),
-        in_specs=[vmem] * 3,
-        out_specs=vmem,
+        in_specs=[vmem, vmem, pl.BlockSpec(memory_space=pl.ANY)],
+        out_specs=pl.BlockSpec(memory_space=pl.ANY),
         scratch_shapes=[
+            pltpu.VMEM((rows, cols), bf16),
+            pltpu.VMEM((row_blocks, padded, rows), bf16),
+            pltpu.VMEM((chunks, col_blocks - 1, padded, width), bf16),
+            pltpu.VMEM((chunks, share, width), bf16),
             pltpu.VMEM((row_blocks, padded, rows), bf16),
             pltpu.VMEM((col_blocks - 1, row_blocks, padded, rows), bf16),
             pltpu.VMEM((depth, rows), jnp.float32),
@@ -335,6 +364,8 @@
             pltpu.VMEM((chunks, rows, width), bf16),
             pltpu.VMEM((chunks, doms - 1, share, width), bf16),
             pltpu.VMEM((chunks, doms - 1, share, width), bf16),
+            pltpu.SemaphoreType.DMA,
+            pltpu.SemaphoreType.DMA((chunks,)),
             pltpu.SemaphoreType.DMA((row_blocks - 1,)),
             pltpu.SemaphoreType.DMA((row_blocks - 1,)),
             pltpu.SemaphoreType.DMA((col_blocks - 1,)),
@@ -350,7 +381,7 @@
             pltpu.SemaphoreType.DMA((chunks, doms - 1)),
         ],
         compiler_params=pltpu.CompilerParams(
-            collective_id=0, has_side_effects=True, vmem_limit_bytes=56 << 20
+            collective_id=0, has_side_effects=True, vmem_limit_bytes=44 << 20
         ),
     )(feats, cots, weights[0, 0])
     return merged[None]

time: 109 us -> 103 us (0.945)
  local copies, waits for them, and re-layouts: 10.8 us -> 5.08 us
    unnamed x5 -> x1, local copies, waits for them, and re-layouts: 6.05 us -> 2.15 us
    reshape x0 -> x2, local copies, waits for them, and re-layouts: none -> 2.93 us  [the longest x1 2.85 us: body(): cots = cotangents[0].transpose(1, 0, 2).reshape(live, col_blocks * cols)]
    another operation x2 -> x0, local copies, waits for them, and re-layouts: 2.6 us -> none  [body(): cots = cotangents[0].reshape(live, col_blocks, chunks, width)]
    transpose x2 -> x0, local copies, waits for them, and re-layouts: 1.96 us -> none  [the longest x1 1.24 us: body(): jnp.pad(cots, ((0, padded - live), (0, 0), (0, 0), (0, 0)))]
    mul x1, other arithmetic: 0.09 us -> 1.18 us  [body(): activations[0].transpose(1, 0, 2) * mask[:, :, None]]
where the time goes in v3:
time: 103 us
  Pallas kernels  96.2 us (93%)
  local copies, waits for them, and re-layouts  5.08 us (5%)
  other arithmetic  1.84 us (2%)
    pallas_call x1, Pallas kernels, body(): pl.pallas_call(functools.partial(kernel, doms, row_blocks, col_blocks, li...  96.2 us
    reshape x1, local copies, waits for them, and re-layouts, body(): cots = cotangents[0].transpose(1, 0, 2).reshape(live, col_blocks * cols)  2.85 us
    unnamed x1, local copies, waits for them, and re-layouts  2.15 us

profile of v3, /device:TPU:0, one launch (start us, length us, event | category | flops | bytes accessed | tf_op | source)
XLA Modules:
  0.0 103.2 jit_solution(11510620735742130433)
XLA Ops:
  0.0 0.7 fusion
  0.7 1.2 %bitcast_multiply_fusion = bf16[20,2,2560]{2,1,0:T(2,128)(2,1)S(1)} fusion(bf16[1,2,20,2560]{3,1,2,0:T(2,128)(2,1)} %param.5, bf16[20,2]{1,0:T(8,128)(2,1)S(1)} %fusion), kind=kLoop, calls=%fused_computation | loop fusion | flops 102400 | bytes 409680 | tf_op jit(solution)/shard_map/mul | solution.py:341
  1.8 0.1 reshape.28.feats
  1.9 2.9 %reshape.29.cots = bf16[40,14336]{1,0:T(8,128)(2,1)S(1)} reshape(bf16[20,2,14336]{2,1,0:T(2,128)(2,1)} %bitcast.12) | data formatting | bytes 2293760 | tf_op jit(solution)/shard_map/reshape | solution.py:342
  4.8 96.2 %shard_map.46 = bf16[640,3584]{1,0:T(8,128)(2,1)S(1)} custom-call(bf16[40,2560]{1,0:T(8,128)(2,1)S(1)} %reshape.28.feats, bf16[40,14336]{1,0:T(8,128)(2,1)S(1)} %reshape.29.cots, bf16[640,3584]{1,0:T(8,128)(2,1)} %bitcast.11), custom_call_target="tpu_custom_call" | custom-call | tf_op jit(solution)/shard_map/pallas_call | solution.py:347
  101.0 2.1 %copy.6 = bf16[1,640,3584]{2,1,0:T(8,128)(2,1)} copy(bf16[1,640,3584]{2,1,0:T(8,128)(2,1)S(1)} %bitcast.10) | data formatting | bytes 9175040

commit v4 on v3

--- a/solution.py
+++ b/solution.py
@@ -22,11 +22,13 @@
     chunks, _, tokens, width = held.shape
     batches, rows, depth = feat_cols.shape
     share = rows // doms
-    tile = 128 if rows % 128 == 0 else rows
+    tile = 320 if share % 320 == 0 else share
     piece = 64 if share % 64 == 0 else share
     strip = 128 if depth % 128 == 0 else depth
     last = row_blocks - 1
     cols = chunks * width
+    parts, _, thin = numer.shape
+    halves = parts // chunks
     padded = pieces.shape[2]
 
     def fetch():
@@ -94,12 +96,13 @@
 
     def pad(part):
         if padded == live:
-            return part
+            return part.astype(jnp.bfloat16)
         blank = jnp.zeros((padded - live, part.shape[1]), jnp.float32)
         return jnp.concatenate([part.astype(jnp.float32), blank], axis=0).astype(jnp.bfloat16)
 
     def cot_part(chunk, block):
-        return cots[:, pl.ds(pl.multiple_of(block * cols + chunk * width, width), width)]
+        where = pl.ds(pl.multiple_of(block * cols + chunk * width, width), width)
+        return jnp.concatenate([cots[batch, :, where].astype(jnp.float32) for batch in range(batches)], axis=0)
 
     def feat_part(block):
         return pad(feats[:, pl.ds(pl.multiple_of(block * rows, rows), rows)])
@@ -124,7 +127,7 @@
             here = pl.ds(pl.multiple_of(at * strip, strip), strip)
             turned = feat_rows[here].T
             token = lax.broadcasted_iota(jnp.int32, (rows, strip), 1) + at * strip
-            owner = lax.rem(lax.rem(token, live), batches)
+            owner = lax.div(lax.rem(token, live), live // batches)
             for batch in range(batches):
                 feat_cols[batch, :, here] = jnp.where(owner == batch, turned, 0.0).astype(jnp.bfloat16)
 
@@ -156,7 +159,7 @@
 
     def place(owner, chunk):
         return out.at[
-            pl.ds(pl.multiple_of(owner * share, share), share), pl.ds(pl.multiple_of(chunk * width, width), width)
+            pl.ds(pl.multiple_of(owner * share, share), share), pl.ds(pl.multiple_of(chunk * thin, thin), thin)
         ]
 
     def keep(chunk):
@@ -176,13 +179,14 @@
         where = place(lax.rem(dom + slot + 1, doms), chunk)
         return pltpu.make_async_copy(where, where, out_recv.at[chunk, slot])
 
-    def compute(chunk):
-        columns = pl.ds(pl.multiple_of(chunk * width, width), width)
-
-        @pl.loop(0, rows // tile)
+    def compute(whole, half, owner):
+        chunk = whole * halves + half
+        columns = pl.ds(pl.multiple_of(chunk * thin, thin), thin)
+
+        @pl.loop(0, share // tile)
         def _(at):
-            here = pl.ds(pl.multiple_of(at * tile, tile), tile)
-            right = held[chunk].reshape(depth, width)
+            here = pl.ds(pl.multiple_of(owner * share + at * tile, tile), tile)
+            right = held[whole, :, :, half * thin : (half + 1) * thin].reshape(depth, thin)
             total = None
             for batch in range(batches):
                 grad = jnp.dot(feat_cols[batch, here], right, preferred_element_type=jnp.float32)
@@ -242,6 +246,19 @@
             for peer_step in range(1, col_blocks):
                 feat_across(peer_step).start()
 
+        for half in range(halves):
+            before = (step - row_blocks) * halves + half
+
+            @pl.when(jnp.logical_and(before >= 0, before < parts))
+            def _():
+                for slot in range(doms - 1):
+                    for which in range(2):
+                        term_arrival(before, slot, which).wait()
+                merge(before)
+                keep(before).start()
+                for peer_step in range(1, doms):
+                    out_copy(before, peer_step).start()
+
         for far in range(1, row_blocks):
             chunk = step - far
 
@@ -270,24 +287,16 @@
             turn_feats()
             fetch().wait()
 
-        @pl.when(inside(ready))
-        def _():
-            compute(ready)
-            for peer_step in range(1, doms):
-                for which in range(2):
-                    term_copy(ready, peer_step, which).start()
-
-        before = ready - 1
-
-        @pl.when(inside(before))
-        def _():
-            for slot in range(doms - 1):
-                for which in range(2):
-                    term_arrival(before, slot, which).wait()
-            merge(before)
-            keep(before).start()
-            for peer_step in range(1, doms):
-                out_copy(before, peer_step).start()
+        for half in range(halves):
+            part = ready * halves + half
+
+            @pl.when(inside(ready))
+            def _():
+                for peer_step in range(1, doms):
+                    compute(ready, half, lax.rem(dom + peer_step, doms))
+                    for which in range(2):
+                        term_copy(part, peer_step, which).start()
+                compute(ready, half, dom)
 
     for step in range(1, row_blocks):
         feat_along(step).wait_send()
@@ -307,6 +316,8 @@
             def _():
                 hop(chunk, source, down_sem, -1).wait_send()
 
+    @pl.loop(0, parts)
+    def _(chunk):
         for peer_step in range(1, doms):
             for which in range(2):
                 term_copy(chunk, peer_step, which).wait_send()
@@ -317,7 +328,7 @@
 
 
 def chunk_width(cols):
-    for width in (256, 128):
+    for width in (512, 256, 128):
         if cols % width == 0:
             return width
     return cols
@@ -332,14 +343,16 @@
     col_blocks = devices // row_blocks
     width = chunk_width(cols)
     chunks = cols // width
+    halves = 2 if width % 256 == 0 else 1
+    parts, thin = chunks * halves, width // halves
     tokens = col_blocks * batches * slots
     depth = row_blocks * tokens
 
-    mask = (jnp.arange(slots)[:, None] < lengths[0, :, 0][None, :]).astype(jnp.bfloat16)
+    mask = (jnp.arange(slots)[None, :] < lengths[0, :, 0:1]).astype(jnp.bfloat16)
     live = batches * slots
     padded = -(-live // 16) * 16
-    feats = (activations[0].transpose(1, 0, 2) * mask[:, :, None]).reshape(live, row_blocks * rows)
-    cots = cotangents[0].transpose(1, 0, 2).reshape(live, col_blocks * cols)
+    feats = (activations[0] * mask[:, :, None]).reshape(live, row_blocks * rows)
+    cots = cotangents[0]
 
     share = rows // doms
     vmem = pl.BlockSpec(memory_space=pltpu.VMEM)
@@ -353,19 +366,19 @@
             pltpu.VMEM((rows, cols), bf16),
             pltpu.VMEM((row_blocks, padded, rows), bf16),
             pltpu.VMEM((chunks, col_blocks - 1, padded, width), bf16),
-            pltpu.VMEM((chunks, share, width), bf16),
+            pltpu.VMEM((parts, share, thin), bf16),
             pltpu.VMEM((row_blocks, padded, rows), bf16),
             pltpu.VMEM((col_blocks - 1, row_blocks, padded, rows), bf16),
             pltpu.VMEM((depth, rows), jnp.float32),
             pltpu.VMEM((batches, rows, depth), bf16),
             pltpu.VMEM((chunks, col_blocks - 1, padded, width), bf16),
             pltpu.VMEM((chunks, row_blocks, tokens, width), bf16),
-            pltpu.VMEM((chunks, rows, width), bf16),
-            pltpu.VMEM((chunks, rows, width), bf16),
-            pltpu.VMEM((chunks, doms - 1, share, width), bf16),
-            pltpu.VMEM((chunks, doms - 1, share, width), bf16),
+            pltpu.VMEM((parts, rows, thin), bf16),
+            pltpu.VMEM((parts, rows, thin), bf16),
+            pltpu.VMEM((parts, doms - 1, share, thin), bf16),
+            pltpu.VMEM((parts, doms - 1, share, thin), bf16),
             pltpu.SemaphoreType.DMA,
-            pltpu.SemaphoreType.DMA((chunks,)),
+            pltpu.SemaphoreType.DMA((parts,)),
             pltpu.SemaphoreType.DMA((row_blocks - 1,)),
             pltpu.SemaphoreType.DMA((row_blocks - 1,)),
             pltpu.SemaphoreType.DMA((col_blocks - 1,)),
@@ -375,10 +388,10 @@
             pltpu.SemaphoreType.DMA((chunks, row_blocks)),
             pltpu.SemaphoreType.DMA((chunks, row_blocks)),
             pltpu.SemaphoreType.DMA((chunks, row_blocks)),
-            pltpu.SemaphoreType.DMA((chunks, doms - 1, 2)),
-            pltpu.SemaphoreType.DMA((chunks, doms - 1, 2)),
-            pltpu.SemaphoreType.DMA((chunks, doms - 1)),
-            pltpu.SemaphoreType.DMA((chunks, doms - 1)),
+            pltpu.SemaphoreType.DMA((parts, doms - 1, 2)),
+            pltpu.SemaphoreType.DMA((parts, doms - 1, 2)),
+            pltpu.SemaphoreType.DMA((parts, doms - 1)),
+            pltpu.SemaphoreType.DMA((parts, doms - 1)),
         ],
         compiler_params=pltpu.CompilerParams(
             collective_id=0, has_side_effects=True, vmem_limit_bytes=44 << 20

time: 103 us -> 97.4 us (0.946)
  Pallas kernels: 96.2 us -> 91.5 us
  other arithmetic: 1.84 us -> 0.81 us
    pallas_call x1, Pallas kernels: 96.2 us -> 91.5 us  [body(): pl.pallas_call(functools.partial(kernel, doms, row_blocks, col_blocks, li...]
    reshape x2 -> x0, local copies, waits for them, and re-layouts: 2.93 us -> none  [the longest x1 2.85 us: body(): cots = cotangents[0].transpose(1, 0, 2).reshape(live, col_blocks * cols)]
    unnamed x1 -> x3, local copies, waits for them, and re-layouts: 2.15 us -> 4.71 us
    mul x1, other arithmetic: 1.18 us -> 0.09 us  [body(): feats = (activations[0] * mask[:, :, None]).reshape(live, row_blocks * rows)]
where the time goes in v4:
time: 97.4 us; the launch traced here: 97.2 us
  Pallas kernels  91.5 us (94%)
  local copies, waits for them, and re-layouts  4.85 us (5%)
    pallas_call x1, Pallas kernels, body(): pl.pallas_call(functools.partial(kernel, doms, row_blocks, col_blocks, li...  91.5 us
    unnamed x3, local copies, waits for them, and re-layouts  4.71 us

profile of v4, /device:TPU:0, one launch (start us, length us, event | category | flops | bytes accessed | tf_op | source)
XLA Modules:
  0.0 97.2 jit_solution(336497560760432543)
XLA Ops:
  0.0 0.7 compare_convert_fusion
  0.7 0.1 reshape.27
  0.8 1.0 copy.7
  1.8 0.1 broadcast_multiply_fusion.feats
  1.9 1.6 %copy.10 = bf16[1,2,20,14336]{3,2,1,0:T(8,128)(2,1)S(1)} copy(bf16[1,2,20,14336]{3,1,2,0:T(2,128)(2,1)} %param.6) | data formatting | bytes 2293760 | tf_op args[2]
  3.5 91.5 %shard_map.46 = bf16[640,3584]{1,0:T(8,128)(2,1)S(1)} custom-call(bf16[40,2560]{1,0:T(8,128)(2,1)S(1)} %broadcast_multiply_fusion.feats, bf16[2,20,14336]{2,1,0:T(8,128)(2,1)S(1)} %bitcast.7, bf16[640,3584]{1,0:T(8,128)(2,1)} %bitcast.8), custom_call_target="tpu_custom_call" | custom-call | tf_op jit(solution)/shard_map/pallas_call | solution.py:360
  95.1 2.1 %copy.12 = bf16[1,640,3584]{2,1,0:T(8,128)(2,1)} copy(bf16[1,640,3584]{2,1,0:T(8,128)(2,1)S(1)} %bitcast.6) | data formatting | bytes 9175040
  (1 shorter events, 0.0 us)

commit v5 on v4

--- a/solution.py
+++ b/solution.py
@@ -211,11 +211,12 @@
         return jnp.logical_and(chunk >= 0, chunk < chunks)
 
     ahead = min(2, chunks)
+    send_pieces(0)
     for step in range(1, row_blocks):
         peer = lax.rem(row + step, row_blocks)
         feat_out[peer] = feat_part(peer)
         feat_along(step).start()
-    for chunk in range(ahead):
+    for chunk in range(1, ahead):
         send_pieces(chunk)
     feat_box[row] = feat_part(row)
 
@@ -239,7 +240,7 @@
             def _():
                 hop(step, row, down_sem, -1).start()
 
-        @pl.when(step == 0)
+        @pl.when(step == 1)
         def _():
             for slot in range(row_blocks - 1):
                 feat_along_arrival(slot).wait()

time: 97.4 us -> 97.4 us (level)
  no operation moved by 1% of the time
where the time goes in v5:
time: 97.4 us; the launch traced here: 97.2 us
  Pallas kernels  91.5 us (94%)
  local copies, waits for them, and re-layouts  4.85 us (5%)
    pallas_call x1, Pallas kernels, body(): pl.pallas_call(functools.partial(kernel, doms, row_blocks, col_blocks, li...  91.5 us
    unnamed x3, local copies, waits for them, and re-layouts  4.71 us

profile of v5, /device:TPU:0, one launch (start us, length us, event | category | flops | bytes accessed | tf_op | source)
XLA Modules:
  0.0 97.2 jit_solution(4874460723353594359)
XLA Ops:
  0.0 0.7 compare_convert_fusion
  0.7 0.1 reshape.27
  0.8 1.0 copy.7
  1.8 0.1 broadcast_multiply_fusion.feats
  1.9 1.6 %copy.10 = bf16[1,2,20,14336]{3,2,1,0:T(8,128)(2,1)S(1)} copy(bf16[1,2,20,14336]{3,1,2,0:T(2,128)(2,1)} %param.6) | data formatting | bytes 2293760 | tf_op args[2]
  3.5 91.5 %shard_map.46 = bf16[640,3584]{1,0:T(8,128)(2,1)S(1)} custom-call(bf16[40,2560]{1,0:T(8,128)(2,1)S(1)} %broadcast_multiply_fusion.feats, bf16[2,20,14336]{2,1,0:T(8,128)(2,1)S(1)} %bitcast.7, bf16[640,3584]{1,0:T(8,128)(2,1)} %bitcast.8), custom_call_target="tpu_custom_call" | custom-call | tf_op jit(solution)/shard_map/pallas_call | solution.py:361
  95.1 2.1 %copy.12 = bf16[1,640,3584]{2,1,0:T(8,128)(2,1)} copy(bf16[1,640,3584]{2,1,0:T(8,128)(2,1)S(1)} %bitcast.6) | data formatting | bytes 9175040
  (1 shorter events, 0.0 us)
